TPU v7x, 32 devices: a whole 2x2x4 slice. The times are simulated.
32 devices in a mesh: groups: 2 (over y), tensor: 4 (over z), dp: 4 (over x, core).
Axes of the slice: x: 2, y: 2, z: 4, core: 2. Of those that a mesh axis runs over, the one named last changes fastest.
Arguments:
- hidden_states: bfloat16 [8, 128, 8192], P(('groups', 'dp'), None, 'tensor'), parts along dimension 0, may hold values from -4 to 4
- norm_gain: bfloat16 [8192], P('tensor'), may hold values from 0.5 to 1.5
- w_query: bfloat16 [8192, 8192], P(None, 'tensor'), may hold values from -0.125 to 0.125
- b_query: bfloat16 [8192], P('tensor'), may hold values from -12 to 12
- w_key: bfloat16 [8192, 1024], P(None, 'tensor'), may hold values from -0.0625 to 0.0625
- b_key: bfloat16 [1024], P('tensor'), may hold values from -4 to 4
- w_value: bfloat16 [8192, 1024], P(None, 'tensor'), may hold values from -0.0625 to 0.0625
- b_value: bfloat16 [1024], P('tensor'), may hold values from -4 to 4
- w_out: bfloat16 [8192, 8192], P('tensor'), may hold values from -0.75 to 0.75
- cache_keys: bfloat16 [8, 16384, 1024], P(('groups', 'dp'), 'tensor'), parts along dimension 0, may hold values from -12.5 to 12.5
- cache_values: bfloat16 [8, 16384, 1024], P(('groups', 'dp'), 'tensor'), parts along dimension 0, may hold values from -6 to 6
- cached_lens: int32 [8], P(('groups', 'dp')), parts along dimension 0, may hold values from 4096 to 16384, as said below
- positions: int32 [8, 128], P(('groups', 'dp')), parts along dimension 0, may hold values from 4096 to 16511, as said below
Outputs:
- hidden_out: bfloat16 [8, 128, 8192], P(('groups', 'dp'), None, 'tensor'), parts along dimension 0
There are 2 independent parts, one for each index of `groups`. A program takes and returns all parts, laid end to end along the dimension named above; an argument that names none is the same for every part. Nothing has to cross between parts.
Inputs may be any that keep to these rules, and one draw needn't show every extreme that they name: `cached_lens`: in every part at least one prompt has exactly 16384 cached positions. positions[p, i] = cached_lens[p] + i.
All inputs are finite; a program needn't handle non-finite values.
Results may differ from a plain program's by a relative error of at most 0.013.
Values may be sent and summed in bfloat16 or wider, within the bound.
A program may use at most 448 MiB of HBM per device.

v0:
```python
import math

import jax
import jax.numpy as jnp
from jax import lax
from jax.sharding import PartitionSpec as P

HD = 128
QB = 128


ROPE_BASE = 1000000.0
NORM_EPS = 1e-06
MASK_FILL = -1e30


def quantize(values):
    biggest = jnp.max(jnp.abs(values), axis=-1)
    block_scale = ((biggest + 1e-06) / 127.0).astype(jnp.bfloat16)
    payload = (values / block_scale.astype(jnp.float32)[..., None]).astype(jnp.bfloat16)
    return (payload, block_scale)


def dequantize(payload, block_scale):
    return payload.astype(jnp.float32) * block_scale.astype(jnp.float32)[..., None]


def rotate_cols(values, token_pos, first_col):
    row_count = values.shape[0]
    pair_count = values.shape[1] // 2
    column = first_col + 2 * jnp.arange(pair_count, dtype=jnp.int32)
    pair_index = column % HD // 2
    inverse = jnp.power(ROPE_BASE, -2.0 * pair_index.astype(jnp.float32) / HD)
    angles = token_pos.astype(jnp.float32)[:, None] * inverse[None, :]
    cosine = jnp.cos(angles)
    sine_part = jnp.sin(angles)
    paired = values.reshape(row_count, pair_count, 2)
    even_part = paired[:, :, 0]
    odd_part = paired[:, :, 1]
    turned = jnp.stack(
        [even_part * cosine - odd_part * sine_part, odd_part * cosine + even_part * sine_part],
        axis=-1,
    )
    return turned.reshape(row_count, pair_count * 2)


def block_terms(queries, keys_all, values_all, allowed):
    scores = jnp.einsum(
        "tgqd,lgd->tgql", queries, keys_all, preferred_element_type=jnp.float32
    ) / math.sqrt(HD)
    visible = allowed[:, None, None, :]
    masked = jnp.where(visible, scores, MASK_FILL)
    block_max = jnp.max(masked, axis=-1)
    exp_terms = jnp.where(visible, jnp.exp(masked - block_max[..., None]), 0.0)
    block_total = jnp.sum(exp_terms, axis=-1)
    summed = jnp.einsum(
        "tgql,lgd->tgqd",
        exp_terms.astype(jnp.bfloat16),
        values_all,
        preferred_element_type=jnp.float32,
    )
    return (block_max, block_total, summed)


def on_device(
    hidden_states,
    norm_gain,
    w_query,
    b_query,
    w_key,
    b_key,
    w_value,
    b_value,
    w_out,
    cache_keys,
    cache_values,
    cached_lens,
    positions,
):
    devices = lax.axis_size("tensor")
    tensor_rank = lax.axis_index("tensor")
    tokens = hidden_states.shape[1]
    feat_dev = hidden_states.shape[2]
    blocks_dev = feat_dev // QB
    full_width = feat_dev * devices
    query_cols = w_query.shape[1]
    kv_cols = w_key.shape[1]
    local_rows = hidden_states[0].astype(jnp.float32)
    payload, block_scale = quantize(local_rows.reshape(tokens, blocks_dev, QB))
    gain_rows = norm_gain.reshape(1, blocks_dev, QB)
    full_pay, full_scale, full_gain = (
        lax.all_gather(payload, "tensor", axis=1, tiled=True),
        lax.all_gather(block_scale, "tensor", axis=1, tiled=True),
        lax.all_gather(gain_rows, "tensor", axis=1, tiled=True),
    )
    restored = dequantize(full_pay, full_scale)
    squares = jnp.sum(restored * restored, axis=(1, 2))
    scaled = (
        (restored * full_gain.astype(jnp.float32)).astype(jnp.bfloat16).reshape(tokens, full_width)
    )
    query_acc = jnp.dot(scaled, w_query, preferred_element_type=jnp.float32)
    key_acc = jnp.dot(scaled, w_key, preferred_element_type=jnp.float32)
    value_acc = jnp.dot(scaled, w_value, preferred_element_type=jnp.float32)
    inv_rms = lax.rsqrt(squares / full_width + NORM_EPS)
    row_scale = inv_rms[:, None]
    token_pos = positions[0]
    query_full = row_scale * query_acc + b_query.astype(jnp.float32)
    key_full = row_scale * key_acc + b_key.astype(jnp.float32)
    query_rot = rotate_cols(query_full, token_pos, tensor_rank * query_cols).astype(jnp.bfloat16)
    key_rot = rotate_cols(key_full, token_pos, tensor_rank * kv_cols).astype(jnp.bfloat16)
    value_new = (row_scale * value_acc + b_value.astype(jnp.float32)).astype(jnp.bfloat16)
    token_ids = jnp.arange(tokens, dtype=jnp.int32)
    cache_count = cache_keys.shape[1]
    per_dev = query_cols // HD
    block_keys, block_values = (
        lax.all_to_all(key_rot, "tensor", split_axis=0, concat_axis=1, tiled=True),
        lax.all_to_all(value_new, "tensor", split_axis=0, concat_axis=1, tiled=True),
    )
    all_queries = lax.all_gather(query_rot, "tensor", axis=1, tiled=True)
    kv_heads = block_keys.shape[1] // HD
    head_count = all_queries.shape[1] // HD
    group_size = head_count // kv_heads
    new_count = block_keys.shape[0]
    queries = all_queries.reshape(tokens, kv_heads, group_size, HD)
    keys_all = jnp.concatenate([cache_keys[0], block_keys], axis=0).reshape(
        cache_count + new_count, kv_heads, HD
    )
    values_all = jnp.concatenate([cache_values[0], block_values], axis=0).reshape(
        cache_count + new_count, kv_heads, HD
    )
    cache_pos = tensor_rank * cache_count + jnp.arange(cache_count, dtype=jnp.int32)
    new_pos = tensor_rank * new_count + jnp.arange(new_count, dtype=jnp.int32)
    allowed = jnp.concatenate(
        [
            jnp.broadcast_to((cache_pos < cached_lens[0])[None, :], (tokens, cache_count)),
            new_pos[None, :] <= token_ids[:, None],
        ],
        axis=1,
    )
    block_max, block_total, summed = block_terms(queries, keys_all, values_all, allowed)
    acc_send = summed.reshape(tokens, devices, per_dev * HD)
    max_send = block_max.reshape(tokens, devices, per_dev)
    tot_send = block_total.reshape(tokens, devices, per_dev)
    acc_in = lax.all_to_all(acc_send, "tensor", split_axis=1, concat_axis=1, tiled=True)
    max_in = lax.all_to_all(max_send, "tensor", split_axis=1, concat_axis=1, tiled=True)
    tot_in = lax.all_to_all(tot_send, "tensor", split_axis=1, concat_axis=1, tiled=True)
    count_rows = acc_in.shape[0]
    top_max = jnp.max(max_in, axis=1, keepdims=True)
    factor = jnp.exp(max_in - top_max)
    numerator = jnp.sum(
        acc_in.reshape(count_rows, devices, per_dev, HD) * factor[..., None], axis=1
    )
    denominator = jnp.sum(factor * tot_in, axis=1)
    attended = (
        (numerator / denominator[..., None]).astype(jnp.bfloat16).reshape(count_rows, per_dev * HD)
    )
    projected = jnp.dot(attended, w_out, preferred_element_type=jnp.float32)
    out_pay, out_scale = quantize(projected.reshape(count_rows, full_width // QB, QB))
    recv_pay, recv_scale = (
        lax.all_to_all(out_pay, "tensor", split_axis=1, concat_axis=0, tiled=True),
        lax.all_to_all(out_scale, "tensor", split_axis=1, concat_axis=0, tiled=True),
    )
    summed_in = jnp.sum(
        dequantize(recv_pay, recv_scale).reshape(devices, tokens, blocks_dev, QB), axis=0
    )
    result = (local_rows + summed_in.reshape(tokens, feat_dev)).astype(jnp.bfloat16)
    return result[None]


def solution(mesh):
    return jax.shard_map(
        on_device,
        mesh=mesh,
        in_specs=(
            P(("groups", "dp"), None, "tensor"),
            P("tensor"),
            P(None, "tensor"),
            P("tensor"),
            P(None, "tensor"),
            P("tensor"),
            P(None, "tensor"),
            P("tensor"),
            P("tensor", None),
            P(("groups", "dp"), "tensor", None),
            P(("groups", "dp"), "tensor", None),
            P(("groups", "dp")),
            P(("groups", "dp"), None),
        ),
        out_specs=P(("groups", "dp"), None, "tensor"),
        check_vma=False,
    )
```

profile of v0, /device:TPU:2, one launch (start us, length us, event | category | flops | bytes accessed | tf_op | source)
XLA Modules:
  0.0 496.3 jit_solution(4515782609874113981)
XLA Ops:
  6.5 1.1 convert_bitcast_fusion.1
  7.7 0.2 copy.94
  7.9 0.3 abs_reduce_fusion.1
  8.2 0.1 copy.62
  8.3 0.1 copy.63
  8.4 1.1 divide_convert_fusion.2
  9.6 0.0 all-gather.5.cloned.1.call-start
  9.6 13.5 %all_gather.13 = bf16[128,64]{0,1:T(8,128)(2,1)S(1)} all-gather(bf16[128,16]{0,1:T(8,128)(2,1)S(1)} %multiply_convert_fusion.2), channel_id=1, replica_groups=mesh['groups'=2,'tensor'=4,'dp'=4] {'tensor'}, dimensions={1}, use_global_device_ids=true | all-gather | bytes 20480 | tf_op jit(solution)/shard_map/all_gather | solution.py:93
  23.1 0.1 copy.64
  23.2 0.7 convert_element_type.164
  23.9 14.1 %all_gather.14 = bf16[1,64,128]{2,1,0:T(8,128)(2,1)S(1)} all-gather(bf16[1,16,128]{2,1,0:T(8,128)(2,1)} %bitcast.124), channel_id=1, replica_groups=mesh['groups'=2,'tensor'=4,'dp'=4] {'tensor'}, dimensions={1}, use_global_device_ids=true | all-gather | bytes 20480 | tf_op jit(solution)/shard_map/all_gather | solution.py:94
  38.0 0.7 convert_bitcast_fusion.3
  38.6 18.9 %all-gather.3.cloned.1.call-done = bf16[128,64,128]{2,1,0:T(8,128)(2,1)} async-done(((bf16[128,16,128]{2,1,0:T(8,128)(2,1)}), bf16[128,64,128]{2,1,0:T(8,128)(2,1)}) %all-gather.3.cloned.1.call-update) | async-done | bytes 2097168 | tf_op jit(solution)/shard_map/all_gather | solution.py:92
  57.5 4.1 multiply_reduce_fusion
  61.7 14.3 %fusion.14 = f32[128,2048]{1,0:T(8,128)S(1)} fusion(bf16[8192,2048]{1,0:T(8,128)(2,1)} %param.15, bf16[16,8,64,128]{3,2,1,0:T(8,128)(2,1)S(1)} %bitcast.110, f32[2048]{0:T(1024)S(1)} %convert_element_type.164, f32[128]{0:T(128)S(1)} %add_rsqrt_fusion), kind=kOutput, calls=%fused_computation.25 | convolution fusion | flops 4295491584 | bytes 36708864 | tf_op jit(solution)/shard_map/dot_general | solution.py:101
  76.0 1.3 copy.77
  77.3 3.3 fusion.68
  80.5 0.3 copy.93
  80.9 1.2 copy.92
  82.1 2.3 fusion.44
  84.4 0.1 pad_maximum_fusion
  84.5 1.1 copy.80
  86.3 11.8 %copy.68 = bf16[1,4096,1024]{1,2,0:T(8,128)(2,1)} copy(bf16[1,4096,1024]{2,1,0:T(8,128)(2,1)} %param.22) | data formatting | bytes 16777216 | tf_op args[9]
  98.1 12.0 %copy.75 = bf16[4096,8,128]{2,0,1:T(8,128)(2,1)} copy(bf16[4096,8,128]{0,2,1:T(8,128)(2,1)} %bitcast.108) | data formatting | bytes 16777216 | tf_op jit(solution)/shard_map/concatenate | solution.py:125
  110.2 0.1 iota_compare_fusion
  110.3 3.9 pad_add_fusion
  114.2 3.6 fusion.32
  117.8 0.1 copy.69
  117.9 0.1 fusion.69
  118.0 0.1 copy.91
  118.1 0.1 copy.90
  118.2 0.3 fusion.52
  118.6 0.1 copy.72
  118.7 0.2 convert_element_type.163
  118.8 0.8 copy.73
  119.6 3.5 all-to-all-start.1
  123.1 4.2 fusion.35
  127.3 3.2 all-to-all-done.1
  130.5 3.3 all-to-all-start
  133.8 0.1 copy.74
  133.9 0.0 all-gather.5.cloned.1.call-done
  133.9 50.6 %fusion = (f32[128,8,8]{0,2,1:T(8,128)}, f32[8,4128,128,8]{2,1,3,0:T(8,128)}) fusion(pred[128,4128]{0,1:T(8,128)(4,1)S(1)} %pad_add_fusion, bf16[128,8,8,128]{0,3,2,1:T(8,128)(2,1)} %bitcast.125, bf16[32,8,128]{2,0,1:T(8,128)(2,1)S(1)} %copy.76, bf16[4096,8,128]{2,0,1:T(8,128)(2,1)} %copy.75), kind=kOutput, calls=%fused_computation.2 | convolution fusion | flops 8775393280 | bytes 146378752 | tf_op jit(solution)/shard_map/tgqd,lgd->tgql/dot_general | solution.py:48
  184.6 42.2 %fusion.1 = f32[128,8,8]{0,2,1:T(8,128)} fusion(f32[8,4128,128,8]{2,1,3,0:T(8,128)} %get-tuple-element.20, f32[128,8,8]{0,2,1:T(8,128)} %get-tuple-element.19, pred[128,4128]{0,1:T(8,128)(4,1)S(1)} %pad_add_fusion), kind=kLoop, calls=%fused_computation.3 | loop fusion | flops 169074688 | bytes 135860224 | tf_op jit(solution)/shard_map/reduce_sum | solution.py:55
  226.8 5.1 %all-to-all-start.4 = ((f32[128,4,16]{0,2,1:T(8,128)}), f32[128,4,16]{0,2,1:T(8,128)S(1)}, u32[]{:S(2)}, u32[]{:S(2)}) async-start(f32[128,4,16]{0,2,1:T(8,128)} %bitcast.23), calls=%async_computation.4 | async-start | bytes 65536 | tf_op jit(solution)/shard_map/all_to_all | solution.py:146
  231.8 11.3 %copy.61 = bf16[1,4096,1024]{1,2,0:T(8,128)(2,1)} copy(bf16[1,4096,1024]{2,1,0:T(8,128)(2,1)} %param.23) | data formatting | bytes 16777216 | tf_op args[10]
  243.1 12.0 %copy.66 = bf16[4096,8,128]{2,0,1:T(8,128)(2,1)} copy(bf16[4096,8,128]{0,2,1:T(8,128)(2,1)} %bitcast.109) | data formatting | bytes 16777216 | tf_op jit(solution)/shard_map/concatenate | solution.py:128
  255.1 0.1 copy.65
  255.2 5.1 %all-to-all-start.3 = ((f32[128,4,16]{0,2,1:T(8,128)}), f32[128,4,16]{0,2,1:T(8,128)S(1)}, u32[]{:S(2)}, u32[]{:S(2)}) async-start(f32[128,4,16]{0,2,1:T(8,128)} %bitcast.20), calls=%async_computation.3 | async-start | bytes 65536 | tf_op jit(solution)/shard_map/all_to_all | solution.py:145
  260.3 50.4 %fusion.3 = f32[8,128,128,8]{2,1,3,0:T(8,128)} fusion(f32[8,4128,128,8]{2,1,3,0:T(8,128)} %get-tuple-element.20, f32[128,8,8]{0,2,1:T(8,128)} %get-tuple-element.19, pred[128,4128]{0,1:T(8,128)(4,1)S(1)} %pad_add_fusion, bf16[32,8,128]{2,0,1:T(8,128)(2,1)S(1)} %copy.67, bf16[4096,8,128]{2,0,1:T(8,128)(2,1)} %copy.66), kind=kOutput, calls=%fused_computation.5 | convolution fusion | flops 8843034624 | bytes 148475904 | tf_op jit(solution)/shard_map/tgql,lgd->tgqd/dot_general | solution.py:56
  310.7 5.1 %all-to-all-start.2 = ((f32[128,4,2048]{0,2,1:T(8,128)}), f32[128,4,2048]{0,2,1:T(8,128)}, u32[]{:S(2)}, u32[]{:S(2)}) async-start(f32[128,4,2048]{0,2,1:T(8,128)} %bitcast.117), calls=%async_computation.2 | async-start | bytes 8388608 | tf_op jit(solution)/shard_map/all_to_all | solution.py:144
  315.8 44.4 %copy.89 = bf16[8192,2048]{1,0:T(8,128)(2,1)} copy(bf16[8192,2048]{0,1:T(8,128)(2,1)} %bitcast.107) | data formatting | bytes 67108864 | tf_op jit(solution)/shard_map/dot_general | solution.py:157
  360.2 47.2 %all-to-all-done.2 = f32[128,4,2048]{0,2,1:T(8,128)} async-done(((f32[128,4,2048]{0,2,1:T(8,128)}), f32[128,4,2048]{0,2,1:T(8,128)}, u32[]{:S(2)}, u32[]{:S(2)}) %all-to-all-start.2) | async-done | bytes 4194336 | tf_op jit(solution)/shard_map/all_to_all | solution.py:144
  407.4 2.6 fusion.13
  410.0 0.1 divide_convert_fusion.1
  410.1 16.4 %abs_reduce_fusion = (f32[128,64]{0,1:T(8,128)S(1)}, f32[128,64,128]{0,2,1:T(8,128)}) fusion(bf16[128,2048,1]{0,1,2:T(8,128)(2,1)S(1)} %bitcast.119, bf16[64,128,2048]{2,1,0:T(8,128)(2,1)} %bitcast.106), kind=kOutput, calls=%fused_computation.20 | convolution fusion | flops 4297056256 | bytes 38305792 | tf_op jit(solution)/shard_map/dot_general | solution.py:157
  426.5 0.6 fusion.67
  427.1 3.3 all-to-all-start.6
  430.4 4.1 divide_convert_fusion
  434.5 1.5 all-to-all-done.6
  436.0 3.6 all-to-all-start.5
  439.6 47.1 %all-to-all-done.5 = bf16[128,64,128]{0,2,1:T(8,128)(2,1)S(1)} async-done(((bf16[128,64,128]{0,2,1:T(8,128)(2,1)}), bf16[128,64,128]{0,2,1:T(8,128)(2,1)S(1)}, u32[]{:S(2)}, u32[]{:S(2)}) %all-to-all-start.5) | async-done | bytes 2097184 | tf_op jit(solution)/shard_map/all_to_all | solution.py:160
  486.6 0.5 fusion.12
  487.2 0.3 copy.84
  487.5 1.9 fusion.38
  (28 shorter events, 0.3 us)
Async XLA Ops:
  6.5 51.0 %all-gather.3.cloned.1.call-start = ((), (), s32[]{:S(2)}) async-start(), calls=%async_computation.7 | async-start | bytes 2621440 | tf_op jit(solution)/shard_map/all_gather | solution.py:92
  9.6 124.3 %all-gather.5.cloned.1.call-start = ((), (), s32[]{:S(2)}) async-start(), calls=%async_computation.8 | async-start | bytes 2621440 | tf_op jit(solution)/shard_map/all_gather | solution.py:119
  76.0 10.3 %copy-start = (bf16[256]{0:T(256)(128)(2,1)S(1)}, bf16[256]{0:T(256)(128)(2,1)}, u32[]{:S(2)}) copy-start(bf16[256]{0:T(256)(128)(2,1)} %param.18) | copy-start | bytes 1540
  98.1 12.0 %copy-start.1 = (bf16[256]{0:T(256)(128)(2,1)S(1)}, bf16[256]{0:T(256)(128)(2,1)}, u32[]{:S(2)}) copy-start(bf16[256]{0:T(256)(128)(2,1)} %param.20) | copy-start | bytes 1540
  119.6 10.9 %all-to-all-start.1 = ((bf16[4,32,256]{2,1,0:T(8,128)(2,1)}), bf16[4,32,256]{2,1,0:T(8,128)(2,1)S(1)}, u32[]{:S(2)}, u32[]{:S(2)}) async-start(bf16[4,32,256]{2,1,0:T(8,128)(2,1)} %copy.73), calls=%async_computation.1 | async-start | bytes 131072 | tf_op jit(solution)/shard_map/all_to_all | solution.py:116
  130.5 96.3 %all-to-all-start = ((bf16[4,32,256]{2,1,0:T(8,128)(2,1)}), bf16[4,32,256]{2,1,0:T(8,128)(2,1)S(1)}, u32[]{:S(2)}, u32[]{:S(2)}) async-start(bf16[4,32,256]{2,1,0:T(8,128)(2,1)} %bitcast.3), calls=%async_computation | async-start | bytes 131072 | tf_op jit(solution)/shard_map/all_to_all | solution.py:117
  226.8 28.4 %all-to-all-start.4 = ((f32[128,4,16]{0,2,1:T(8,128)}), f32[128,4,16]{0,2,1:T(8,128)S(1)}, u32[]{:S(2)}, u32[]{:S(2)}) async-start(f32[128,4,16]{0,2,1:T(8,128)} %bitcast.23), calls=%async_computation.4 | async-start | bytes 65536 | tf_op jit(solution)/shard_map/all_to_all | solution.py:146
  255.2 55.5 %all-to-all-start.3 = ((f32[128,4,16]{0,2,1:T(8,128)}), f32[128,4,16]{0,2,1:T(8,128)S(1)}, u32[]{:S(2)}, u32[]{:S(2)}) async-start(f32[128,4,16]{0,2,1:T(8,128)} %bitcast.20), calls=%async_computation.3 | async-start | bytes 65536 | tf_op jit(solution)/shard_map/all_to_all | solution.py:145
  310.7 96.7 %all-to-all-start.2 = ((f32[128,4,2048]{0,2,1:T(8,128)}), f32[128,4,2048]{0,2,1:T(8,128)}, u32[]{:S(2)}, u32[]{:S(2)}) async-start(f32[128,4,2048]{0,2,1:T(8,128)} %bitcast.117), calls=%async_computation.2 | async-start | bytes 8388608 | tf_op jit(solution)/shard_map/all_to_all | solution.py:144
  427.1 8.8 %all-to-all-start.6 = ((bf16[128,4,16]{0,2,1:T(8,128)(2,1)}), bf16[128,4,16]{0,2,1:T(8,128)(2,1)S(1)}, u32[]{:S(2)}, u32[]{:S(2)}) async-start(bf16[128,4,16]{0,2,1:T(8,128)(2,1)} %bitcast.30), calls=%async_computation.6 | async-start | bytes 32768 | tf_op jit(solution)/shard_map/all_to_all | solution.py:161
  436.0 50.7 %all-to-all-start.5 = ((bf16[128,64,128]{0,2,1:T(8,128)(2,1)}), bf16[128,64,128]{0,2,1:T(8,128)(2,1)S(1)}, u32[]{:S(2)}, u32[]{:S(2)}) async-start(bf16[128,64,128]{0,2,1:T(8,128)(2,1)} %divide_convert_fusion), calls=%async_computation.5 | async-start | bytes 4194304 | tf_op jit(solution)/shard_map/all_to_all | solution.py:160
Sparse Core Ops, SparseCore 0:
  9.7 47.7 all-gather.2
  85.7 45.4 all-gather.4
where the time goes:
time: 500 us; the launch traced here: 496 us
  matrix products  140 us (28%)
  waiting for transfers between devices  118 us (24%)
  local copies, waits for them, and re-layouts  101 us (20%)
  other arithmetic  67 us (13%)
  starting transfers between devices  28.9 us (6%)
  blocking collectives  27.5 us (6%)
  between operations  14.4 us (3%)
    dot_general x1, matrix products, block_terms(): jnp.einsum('tgqd,lgd->tgql', queries, keys_all, preferred_element_type=jn...  50.6 us
    dot_general x1, matrix products, block_terms(): jnp.einsum('tgql,lgd->tgqd', exp_terms.astype(jnp.bfloat16), values_all,...  50.4 us
    all_to_all x1, waiting for transfers between devices, on_device(): lax.all_to_all(acc_send, 'tensor', split_axis=1, concat_axis=1, tiled=True)  47.2 us
    all_to_all x1, waiting for transfers between devices, on_device(): lax.all_to_all(out_pay, 'tensor', split_axis=1, concat_axis=0, tiled=True)  47.1 us
    dot_general x1, local copies, waits for them, and re-layouts, on_device(): projected = jnp.dot(attended, w_out, preferred_element_type=jnp.float32)  44.4 us
    reduce_sum x1, other arithmetic, block_terms(): block_total = jnp.sum(exp_terms, axis=-1)  42.2 us
    unnamed x11, local copies, waits for them, and re-layouts  25.1 us
    all_gather x1, waiting for transfers between devices, on_device(): lax.all_gather(payload, 'tensor', axis=1, tiled=True)  18.9 us
  transfers between devices with their start and end apart: 9, of which 5 were waited for; matrix products, arithmetic and copies ran while one was open for 51% of the time, Pallas kernels for 0%

commit v1 on v0

v1 whole, which is shorter than its diff:
```python
import functools
import math

import jax
import jax.numpy as jnp
from jax import lax
from jax.experimental import pallas as pl
from jax.experimental.pallas import tpu as pltpu
from jax.sharding import PartitionSpec as P

HD = 128
QB = 128


ROPE_BASE = 1000000.0
NORM_EPS = 1e-06
MASK_FILL = -1e30
LOG2E = 1.4426950408889634
TILE_ROWS = 256


def quantize(values):
    biggest = jnp.max(jnp.abs(values), axis=-1)
    block_scale = ((biggest + 1e-06) / 127.0).astype(jnp.bfloat16)
    payload = (values / block_scale.astype(jnp.float32)[..., None]).astype(jnp.bfloat16)
    return (payload, block_scale)


def dequantize(payload, block_scale):
    return payload.astype(jnp.float32) * block_scale.astype(jnp.float32)[..., None]


def rotation_tables(token_pos):
    column = jnp.arange(HD, dtype=jnp.int32)
    pair_index = column // 2
    inverse = jnp.power(ROPE_BASE, -2.0 * pair_index.astype(jnp.float32) / HD)
    angles = token_pos.astype(jnp.float32)[:, None] * inverse[None, :]
    sign = jnp.where(column % 2 == 0, -1.0, 1.0)
    return jnp.cos(angles), jnp.sin(angles) * sign[None, :]


def fit_table(table, first_col, cols):
    if cols >= HD:
        return jnp.tile(table, (1, cols // HD))
    return lax.dynamic_slice_in_dim(table, first_col % HD, cols, 1)


def rotate_cols(values, cosine, sine):
    even = jnp.arange(values.shape[1], dtype=jnp.int32) % 2 == 0
    swapped = jnp.where(even[None, :], jnp.roll(values, -1, axis=1), jnp.roll(values, 1, axis=1))
    return values * cosine + swapped * sine


def attend_kernel(group, cache_tile, info, q_ref, k_ref, v_ref, nk_ref, nv_ref, acc_ref, stat_ref, s0, s1):
    head = pl.program_id(0)
    tokens = q_ref.shape[0]
    cache_count = k_ref.shape[0]
    new_count = nk_ref.shape[0]
    heads_tile = TILE_ROWS // tokens
    tiles = group // heads_tile
    head_count = group * pl.num_programs(0)
    scratch = (s0, s1)
    visible, new_first, new_valid = info[0], info[1], info[2]
    spans = [(lo, min(cache_tile, cache_count - lo)) for lo in range(0, cache_count, cache_tile)]
    nt = (((1,), (1,)), ((), ()))

    def score(tile, buffer):
        queries = jnp.concatenate(
            [q_ref[:, pl.ds((tile * heads_tile + j) * HD, HD)] for j in range(heads_tile)], axis=0
        )
        best = jnp.full((TILE_ROWS, 128), MASK_FILL, jnp.float32)
        for lo, size in spans:
            raw = lax.dot_general(queries, k_ref[pl.ds(lo, size), :], nt, preferred_element_type=jnp.float32)
            place = lo + lax.broadcasted_iota(jnp.int32, (1, size), 1)
            raw = jnp.where(place < visible, raw, MASK_FILL)
            buffer[:, pl.ds(lo, size)] = raw
            for c in range(0, size, 128):
                best = jnp.maximum(best, raw[:, c : c + 128])
        raw = lax.dot_general(queries, nk_ref[...], nt, preferred_element_type=jnp.float32)
        place = lax.broadcasted_iota(jnp.int32, (TILE_ROWS, new_count), 1)
        token = lax.broadcasted_iota(jnp.int32, (TILE_ROWS, new_count), 0) % tokens
        raw = jnp.where((place < new_valid) & (new_first + place <= token), raw, MASK_FILL)
        buffer[:, pl.ds(cache_count, new_count)] = raw
        for c in range(0, new_count, 128):
            best = jnp.maximum(best, raw[:, c : c + 128])
        return jnp.max(best, axis=1, keepdims=True)

    lane = lax.broadcasted_iota(jnp.int32, (tokens, stat_ref.shape[1]), 1)

    def weigh(tile, buffer, top):
        shift = jnp.where(top > 0.5 * MASK_FILL, top, 0.0)
        total = jnp.zeros((TILE_ROWS, 2 * HD), jnp.float32)
        for lo, size in spans + [(cache_count, new_count)]:
            weight = jnp.exp2(buffer[:, pl.ds(lo, size)] - shift).astype(jnp.bfloat16)
            value = v_ref[pl.ds(lo, size), :] if lo < cache_count else nv_ref[...]
            value = jnp.concatenate([value, jnp.ones((size, HD), jnp.bfloat16)], axis=1)
            total += jnp.dot(weight, value, preferred_element_type=jnp.float32)
        for j in range(heads_tile):
            index = tile * heads_tile + j
            rows = slice(j * tokens, (j + 1) * tokens)
            acc_ref[:, pl.ds(index * HD, HD)] = total[rows, :HD].astype(jnp.bfloat16)
            where = head * group + index
            stats = jnp.where(lane == where, jnp.broadcast_to(top[rows], lane.shape), stat_ref[...])
            stat_ref[...] = jnp.where(lane == head_count + where, total[rows, HD : HD + 1], stats)

    @pl.when(head == 0)
    def _():
        stat_ref[...] = jnp.zeros_like(stat_ref)

    top = score(0, scratch[0])
    for tile in range(tiles):
        later = score(tile + 1, scratch[(tile + 1) % 2]) if tile + 1 < tiles else None
        weigh(tile, scratch[tile % 2], top)
        top = later


def attend(queries, cache_k, cache_v, new_k, new_v, info, kv_heads):
    tokens, width = queries.shape
    group = width // HD // kv_heads
    cache_count = cache_k.shape[0]
    new_count = new_k.shape[0]
    return pl.pallas_call(
        functools.partial(attend_kernel, group, min(1024, cache_count)),
        grid=(kv_heads,),
        in_specs=[
            pl.BlockSpec(memory_space=pltpu.SMEM),
            pl.BlockSpec((tokens, group * HD), lambda g: (0, g)),
            pl.BlockSpec((cache_count, HD), lambda g: (0, g)),
            pl.BlockSpec((cache_count, HD), lambda g: (0, g)),
            pl.BlockSpec((new_count, HD), lambda g: (0, g)),
            pl.BlockSpec((new_count, HD), lambda g: (0, g)),
        ],
        out_specs=[
            pl.BlockSpec((tokens, group * HD), lambda g: (0, g)),
            pl.BlockSpec((tokens, 2 * width // HD), lambda g: (0, 0)),
        ],
        out_shape=[
            jax.ShapeDtypeStruct((tokens, width), jnp.bfloat16),
            jax.ShapeDtypeStruct((tokens, 2 * width // HD), jnp.float32),
        ],
        scratch_shapes=[pltpu.VMEM((TILE_ROWS, cache_count + new_count), jnp.float32)] * 2,
        compiler_params=pltpu.CompilerParams(vmem_limit_bytes=48 * 1024 * 1024),
        cost_estimate=pl.CostEstimate(
            flops=4 * tokens * width * (cache_count + new_count),
            bytes_accessed=4 * cache_count * kv_heads * HD + 4 * tokens * width,
            transcendentals=tokens * width // HD * (cache_count + new_count),
        ),
    )(info, queries, cache_k, cache_v, new_k, new_v)


def on_device(
    hidden_states,
    norm_gain,
    w_query,
    b_query,
    w_key,
    b_key,
    w_value,
    b_value,
    w_out,
    cache_keys,
    cache_values,
    cached_lens,
    positions,
):
    devices = lax.axis_size("tensor")
    tensor_rank = lax.axis_index("tensor")
    tokens = hidden_states.shape[1]
    feat_dev = hidden_states.shape[2]
    blocks_dev = feat_dev // QB
    full_width = feat_dev * devices
    query_cols = w_query.shape[1]
    kv_cols = w_key.shape[1]
    local_rows = hidden_states[0].astype(jnp.float32)
    payload, block_scale = quantize(local_rows.reshape(tokens, blocks_dev, QB))
    restored = dequantize(payload, block_scale)
    gain_rows = norm_gain.reshape(1, blocks_dev, QB).astype(jnp.float32)
    scaled_dev = (restored * gain_rows).astype(jnp.bfloat16).reshape(tokens, feat_dev)
    squares = lax.psum(jnp.sum(restored * restored, axis=(1, 2)), "tensor")
    scaled = lax.all_gather(scaled_dev, "tensor", axis=1, tiled=True)
    query_acc = jnp.dot(scaled, w_query, preferred_element_type=jnp.float32)
    key_acc = jnp.dot(scaled, w_key, preferred_element_type=jnp.float32)
    value_acc = jnp.dot(scaled, w_value, preferred_element_type=jnp.float32)
    inv_rms = lax.rsqrt(squares / full_width + NORM_EPS)
    row_scale = inv_rms[:, None]
    cosine, sine = rotation_tables(positions[0])
    query_full = row_scale * query_acc + b_query.astype(jnp.float32)
    key_full = row_scale * key_acc + b_key.astype(jnp.float32)
    fold = LOG2E / math.sqrt(HD)
    query_rot = rotate_cols(
        query_full,
        fit_table(cosine * fold, tensor_rank * query_cols, query_cols),
        fit_table(sine * fold, tensor_rank * query_cols, query_cols),
    ).astype(jnp.bfloat16)
    key_rot = rotate_cols(
        key_full,
        fit_table(cosine, tensor_rank * kv_cols, kv_cols),
        fit_table(sine, tensor_rank * kv_cols, kv_cols),
    ).astype(jnp.bfloat16)
    value_new = (row_scale * value_acc + b_value.astype(jnp.float32)).astype(jnp.bfloat16)
    cache_count = cache_keys.shape[1]
    per_dev = query_cols // HD
    block_keys, block_values = (
        lax.all_to_all(key_rot, "tensor", split_axis=0, concat_axis=1, tiled=True),
        lax.all_to_all(value_new, "tensor", split_axis=0, concat_axis=1, tiled=True),
    )
    all_queries = lax.all_gather(query_rot, "tensor", axis=1, tiled=True)
    kv_heads = block_keys.shape[1] // HD
    new_count = block_keys.shape[0]
    pad = -new_count % 128
    info = jnp.stack(
        [cached_lens[0] - tensor_rank * cache_count, tensor_rank * new_count, jnp.int32(new_count)]
    ).astype(jnp.int32)
    sums, stats = attend(
        all_queries,
        cache_keys[0],
        cache_values[0],
        jnp.pad(block_keys, ((0, pad), (0, 0))),
        jnp.pad(block_values, ((0, pad), (0, 0))),
        info,
        kv_heads,
    )
    acc_in = lax.all_to_all(
        sums.reshape(tokens, devices, per_dev * HD), "tensor", split_axis=1, concat_axis=1, tiled=True
    )
    stat_in = lax.all_to_all(
        stats.reshape(tokens, 2, devices, per_dev), "tensor", split_axis=2, concat_axis=2, tiled=True
    )
    max_in, tot_in = stat_in[:, 0], stat_in[:, 1]
    top_max = jnp.max(max_in, axis=1, keepdims=True)
    factor = jnp.exp2(max_in - top_max)
    numerator = jnp.sum(
        acc_in.astype(jnp.float32).reshape(tokens, devices, per_dev, HD) * factor[..., None], axis=1
    )
    denominator = jnp.sum(factor * tot_in, axis=1)
    attended = (
        (numerator / denominator[..., None]).astype(jnp.bfloat16).reshape(tokens, per_dev * HD)
    )
    projected = jnp.dot(attended, w_out, preferred_element_type=jnp.float32)
    out_pay, out_scale = quantize(projected.reshape(tokens, full_width // QB, QB))
    recv_pay, recv_scale = (
        lax.all_to_all(out_pay, "tensor", split_axis=1, concat_axis=0, tiled=True),
        lax.all_to_all(out_scale, "tensor", split_axis=1, concat_axis=0, tiled=True),
    )
    summed_in = jnp.sum(
        dequantize(recv_pay, recv_scale).reshape(devices, tokens, blocks_dev, QB), axis=0
    )
    result = (local_rows + summed_in.reshape(tokens, feat_dev)).astype(jnp.bfloat16)
    return result[None]


def solution(mesh):
    return jax.shard_map(
        on_device,
        mesh=mesh,
        in_specs=(
            P(("groups", "dp"), None, "tensor"),
            P("tensor"),
            P(None, "tensor"),
            P("tensor"),
            P(None, "tensor"),
            P("tensor"),
            P(None, "tensor"),
            P("tensor"),
            P("tensor", None),
            P(("groups", "dp"), "tensor", None),
            P(("groups", "dp"), "tensor", None),
            P(("groups", "dp")),
            P(("groups", "dp"), None),
        ),
        out_specs=P(("groups", "dp"), None, "tensor"),
        check_vma=False,
    )
```

time: 500 us -> 348 us (0.70)
  matrix products: 140 us -> 36.4 us
  Pallas kernels: 0 us -> 63.3 us
  other arithmetic: 67 us -> 17.4 us
  local copies, waits for them, and re-layouts: 101 us -> 59.8 us
  blocking collectives: 27.5 us -> 12.1 us
  starting transfers between devices: 28.9 us -> 22.3 us
    dot_general x2 -> x0, matrix products: 101 us -> none  [the longest x1 50.6 us: block_terms(): jnp.einsum('tgqd,lgd->tgql', queries, keys_all, preferred_element_type=jn...]
    pallas_call x0 -> x1, Pallas kernels: none -> 63.3 us  [attend(): pl.pallas_call(functools.partial(attend_kernel, group, min(1024, cache_co...]
    reduce_sum x3 -> x2, other arithmetic: 48.9 us -> 3.24 us  [the longest x1 2.9 us: on_device(): jnp.sum(acc_in.astype(jnp.float32).reshape(tokens, devices, per_dev, HD)...]
    all_to_all x3 -> x2, waiting for transfers between devices: 47.2 us -> 4.21 us  [the longest x1 4.21 us: on_device(): lax.all_to_all(stats.reshape(tokens, 2, devices, per_dev), 'tensor', spli...]
    all_gather x2 -> x0, blocking collectives: 27.5 us -> none  [the longest x1 14.1 us: on_device(): lax.all_gather(gain_rows, 'tensor', axis=1, tiled=True)]
    concatenate x7 -> x0, local copies, waits for them, and re-layouts: 24.1 us -> none  [the longest x3 12.1 us: on_device(): jnp.concatenate([cache_keys[0], block_keys], axis=0)]
    all_gather x1, waiting for transfers between devices: 0.02 us -> 23.4 us  [on_device(): all_queries = lax.all_gather(query_rot, 'tensor', axis=1, tiled=True)]
    unnamed x11 -> x16, local copies, waits for them, and re-layouts: 25.1 us -> 2 us
  transfers between devices with their start and end apart: 9 -> 8, of which waited for: 5 -> 7; matrix products, arithmetic and copies ran while one was open for 51% -> 19% of each run, Pallas kernels for 0% -> 0%
where the time goes in v1:
time: 348 us; the launch traced here: 344 us
  waiting for transfers between devices  119 us (34%)
  Pallas kernels  63.3 us (18%)
  local copies, waits for them, and re-layouts  59.8 us (17%)
  matrix products  36.4 us (10%)
  starting transfers between devices  22.3 us (6%)
  other arithmetic  17.4 us (5%)
  between operations  14.4 us (4%)
  blocking collectives  12.1 us (3%)
    pallas_call x1, Pallas kernels, attend(): pl.pallas_call(functools.partial(attend_kernel, group, min(1024, cache_co...  63.3 us
    all_to_all x1, waiting for transfers between devices, on_device(): lax.all_to_all(out_pay, 'tensor', split_axis=1, concat_axis=0, tiled=True)  46.1 us
    dot_general x1, local copies, waits for them, and re-layouts, on_device(): projected = jnp.dot(attended, w_out, preferred_element_type=jnp.float32)  44.5 us
    all_gather x1, waiting for transfers between devices, on_device(): scaled = lax.all_gather(scaled_dev, 'tensor', axis=1, tiled=True)  34.3 us
    all_gather x1, waiting for transfers between devices, on_device(): all_queries = lax.all_gather(query_rot, 'tensor', axis=1, tiled=True)  23.4 us
    dot_general x1, matrix products, on_device(): projected = jnp.dot(attended, w_out, preferred_element_type=jnp.float32)  16.4 us
    dot_general x1, matrix products, on_device(): query_acc = jnp.dot(scaled, w_query, preferred_element_type=jnp.float32)  13.5 us
    psum x1, blocking collectives, on_device(): squares = lax.psum(jnp.sum(restored * restored, axis=(1, 2)), 'tensor')  12.1 us
  transfers between devices with their start and end apart: 8, of which 7 were waited for; matrix products, arithmetic and copies ran while one was open for 19% of the time, Pallas kernels for 0%

profile of v1, /device:TPU:2, one launch (start us, length us, event | category | flops | bytes accessed | tf_op | source)
XLA Modules:
  0.0 344.2 jit_solution(5651579294461007924)
XLA Ops:
  6.5 0.7 convert_element_type.166
  7.3 1.1 fusion.6
  8.4 0.0 copy-start.3
  8.5 0.2 copy.61
  8.7 0.0 copy-start.4
  8.7 0.3 reduce_max.27
  9.0 0.1 copy.44
  9.1 0.1 copy.45
  9.2 0.3 div.72
  9.5 1.3 fusion.15
  10.9 0.0 all-gather.3.cloned.1.call-update
  10.9 0.0 all-gather.5.cloned.1.call-start
  10.9 0.2 div.73
  11.1 0.3 multiply_reduce_fusion.1
  11.5 12.1 %psum.7 = f32[128]{0:T(128)S(1)} all-reduce(f32[128]{0:T(128)S(1)} %multiply_reduce_fusion.1), channel_id=1, replica_groups=mesh['groups'=2,'tensor'=4,'dp'=4] {'tensor'}, use_global_device_ids=true, to_apply=%region_2.0 | all-reduce | flops 128 | bytes 1024 | tf_op jit(solution)/shard_map/psum | solution.py:179
  23.6 0.3 multiply_cosine_fusion
  23.9 34.3 %all-gather.3.cloned.1.call-done = bf16[128,8192]{1,0:T(8,128)(2,1)} async-done(((bf16[128,2048]{1,0:T(8,128)(2,1)}), bf16[128,8192]{1,0:T(8,128)(2,1)}) %all-gather.3.cloned.1.call-update) | async-done | bytes 2097168 | tf_op jit(solution)/shard_map/all_gather | solution.py:180
  58.2 13.5 %fusion.2 = f32[128,2048]{1,0:T(8,128)S(1)} fusion(bf16[128,8192]{1,0:T(8,128)(2,1)} %all-gather.3.cloned.1.call-done, bf16[8192,2048]{1,0:T(8,128)(2,1)} %param.15, f32[2048]{0:T(1024)S(1)} %convert_element_type.168, f32[128]{0:T(128)S(1)} %add_rsqrt_fusion), kind=kOutput, calls=%fused_computation.7 | convolution fusion | flops 4295491584 | bytes 36708864 | tf_op jit(solution)/shard_map/dot_general | solution.py:181
  71.7 0.1 fusion.34
  71.8 0.4 fusion.35
  72.2 0.0 copy-start.5
  72.2 0.0 copy-start.6
  72.2 0.1 tile.16
  72.3 0.1 tile.18
  72.3 1.8 fusion.13
  74.2 0.0 all-gather.5.cloned.1.call-update
  74.9 3.5 %fusion.5 = bf16[128,256]{1,0:T(8,128)(2,1)} fusion(bf16[128,8192]{1,0:T(8,128)(2,1)S(1)} %copy-done.1, bf16[8192,256]{1,0:T(8,128)(2,1)} %param.19, f32[256]{0:T(256)S(1)} %convert_element_type.175, f32[128]{0:T(128)S(1)} %add_rsqrt_fusion), kind=kOutput, calls=%fused_computation.17 | convolution fusion | flops 536969216 | bytes 6358528 | tf_op jit(solution)/shard_map/dot_general | solution.py:183
  78.4 3.3 all-to-all-start.1
  81.7 3.0 fusion.4
  84.7 0.1 fusion.36
  84.8 0.1 fusion.37
  85.0 0.7 fusion.17
  85.8 2.8 all-to-all-done.1
  88.5 3.5 %all-to-all-start = ((bf16[4,32,256]{2,1,0:T(8,128)(2,1)}), bf16[4,32,256]{2,1,0:T(8,128)(2,1)S(1)}, u32[]{:S(2)}, u32[]{:S(2)}) async-start(bf16[4,32,256]{2,1,0:T(8,128)(2,1)} %bitcast.7), calls=%async_computation | async-start | bytes 131072 | tf_op jit(solution)/shard_map/all_to_all | solution.py:204
  92.0 0.1 pad_add_fusion.info
  92.1 6.2 %all-to-all-done = bf16[4,32,256]{2,1,0:T(8,128)(2,1)S(1)} async-done(((bf16[4,32,256]{2,1,0:T(8,128)(2,1)}), bf16[4,32,256]{2,1,0:T(8,128)(2,1)S(1)}, u32[]{:S(2)}, u32[]{:S(2)}) %all-to-all-start) | async-done | bytes 65568 | tf_op jit(solution)/shard_map/all_to_all | solution.py:204
  98.4 23.4 %all-gather.5.cloned.1.call-done.q_ref = bf16[128,8192]{1,0:T(8,128)(2,1)} async-done(((bf16[128,2048]{1,0:T(8,128)(2,1)}), bf16[128,8192]{1,0:T(8,128)(2,1)}) %all-gather.5.cloned.1.call-update) | async-done | bytes 2097168 | tf_op jit(solution)/shard_map/all_gather | solution.py:207
  121.8 1.6 copy-done
  123.4 63.3 %shard_map.127 = (bf16[128,8192]{1,0:T(8,128)(2,1)S(1)}, f32[128,128]{1,0:T(8,128)S(1)}) custom-call(s32[3]{0:T(128)S(1)} %pad_add_fusion.info, bf16[128,8192]{1,0:T(8,128)(2,1)S(1)} %copy-done, bf16[4096,1024]{1,0:T(8,128)(2,1)} %bitcast.132, bf16[4096,1024]{1,0:T(8,128)(2,1)} %bitcast.133, bf16[128,1024]{1,0:T(8,128)(2,1)S(1)} %pad.7.nk_ref, ...), custom_call_target="tpu_custom_call" | custom-call | flops 17716740096 | bytes 20971520 | tf_op jit(solution)/shard_map/pallas_call | solution.py:122
  186.7 0.1 copy.49
  186.8 0.6 copy.50
  187.4 3.3 all-to-all-start.3
  190.7 1.5 copy.77
  192.2 4.2 %all-to-all-done.3 = f32[128,2,4,16]{0,3,1,2:T(8,128)S(1)} async-done(((f32[128,2,4,16]{0,3,1,2:T(8,128)}), f32[128,2,4,16]{0,3,1,2:T(8,128)S(1)}, u32[]{:S(2)}, u32[]{:S(2)}) %all-to-all-start.3) | async-done | bytes 65568 | tf_op jit(solution)/shard_map/all_to_all | solution.py:226
  196.4 3.8 %all-to-all-start.2 = ((bf16[128,4,2048]{2,0,1:T(8,128)(2,1)}), bf16[128,4,2048]{2,0,1:T(8,128)(2,1)S(1)}, u32[]{:S(2)}, u32[]{:S(2)}) async-start(bf16[128,4,2048]{2,0,1:T(8,128)(2,1)} %bitcast.118), calls=%async_computation.2 | async-start | bytes 4194304 | tf_op jit(solution)/shard_map/all_to_all | solution.py:223
  200.3 44.5 %copy.56 = bf16[8192,2048]{1,0:T(8,128)(2,1)} copy(bf16[8192,2048]{0,1:T(8,128)(2,1)} %bitcast.116) | data formatting | bytes 67108864 | tf_op jit(solution)/shard_map/dot_general | solution.py:239
  244.7 0.1 copy.53
  244.8 0.1 copy.52
  245.0 2.6 mul.167
  247.6 4.9 %mul.168 = f32[128,4,2048]{2,0,1:T(8,128)} reshape(f32[128,4,16,128]{3,2,0,1:T(8,128)} %mul.167) | data formatting | bytes 8388608 | tf_op jit(solution)/shard_map/mul | solution.py:233
  252.5 2.9 multiply_reduce_fusion
  255.4 0.2 copy.67
  255.6 0.3 fusion.11
  256.0 0.2 reshape.306
  256.2 16.4 %abs_reduce_fusion = (f32[128,64]{0,1:T(8,128)S(1)}, f32[128,64,128]{0,2,1:T(8,128)}) fusion(bf16[128,2048,1]{1,0,2:T(8,128)(2,1)S(1)} %reshape.306, bf16[64,128,2048]{2,1,0:T(8,128)(2,1)} %bitcast.115), kind=kOutput, calls=%fused_computation.4 | convolution fusion | flops 4297056256 | bytes 38305792 | tf_op jit(solution)/shard_map/dot_general | solution.py:239
  272.6 0.6 fusion.32
  273.2 4.8 %all-to-all-start.5 = ((bf16[128,4,16]{0,2,1:T(8,128)(2,1)}), bf16[128,4,16]{0,2,1:T(8,128)(2,1)S(1)}, u32[]{:S(2)}, u32[]{:S(2)}) async-start(bf16[128,4,16]{0,2,1:T(8,128)(2,1)} %bitcast.18), calls=%async_computation.5 | async-start | bytes 32768 | tf_op jit(solution)/shard_map/all_to_all | solution.py:243
  278.0 4.1 %divide_convert_fusion = bf16[128,64,128]{0,2,1:T(8,128)(2,1)} fusion(f32[128,64,128]{0,2,1:T(8,128)} %get-tuple-element.28, f32[128,64]{0,1:T(8,128)S(1)} %get-tuple-element.9), kind=kLoop, calls=%fused_computation.3 | loop fusion | flops 2097152 | bytes 6324224 | tf_op jit(solution)/shard_map/convert_element_type | solution.py:25
  282.1 1.5 all-to-all-done.5
  283.6 3.6 %all-to-all-start.4 = ((bf16[128,64,128]{0,2,1:T(8,128)(2,1)}), bf16[128,64,128]{0,2,1:T(8,128)(2,1)S(1)}, u32[]{:S(2)}, u32[]{:S(2)}) async-start(bf16[128,64,128]{0,2,1:T(8,128)(2,1)} %divide_convert_fusion), calls=%async_computation.4 | async-start | bytes 4194304 | tf_op jit(solution)/shard_map/all_to_all | solution.py:242
  287.2 46.1 %all-to-all-done.4 = bf16[128,64,128]{0,2,1:T(8,128)(2,1)S(1)} async-done(((bf16[128,64,128]{0,2,1:T(8,128)(2,1)}), bf16[128,64,128]{0,2,1:T(8,128)(2,1)S(1)}, u32[]{:S(2)}, u32[]{:S(2)}) %all-to-all-start.4) | async-done | bytes 2097184 | tf_op jit(solution)/shard_map/all_to_all | solution.py:242
  333.4 1.5 fusion.1
  334.9 1.6 copy.55
  336.4 0.9 fusion.8
  (29 shorter events, 0.2 us)
Async XLA Ops:
  6.5 3.0 copy-start.2
  6.5 51.7 %all-gather.3.cloned.1.call-start = ((), (), s32[]{:S(2)}) async-start(), calls=%async_computation.6 | async-start | bytes 2621440 | tf_op jit(solution)/shard_map/all_gather | solution.py:180
  8.4 2.7 copy-start.3
  8.7 14.9 %copy-start.4 = (s32[1,128]{1,0:T(1,128)S(1)}, s32[1,128]{1,0:T(1,128)}, u32[]{:S(2)}) copy-start(s32[1,128]{1,0:T(1,128)} %param.25) | copy-start | bytes 1540
  10.9 110.9 %all-gather.5.cloned.1.call-start = ((), (), s32[]{:S(2)}) async-start(), calls=%async_computation.7 | async-start | bytes 2621440 | tf_op jit(solution)/shard_map/all_gather | solution.py:207
  72.2 2.7 copy-start.5
  72.2 2.7 copy-start.6
  72.2 2.7 copy-start.1
  78.4 10.1 %all-to-all-start.1 = ((bf16[4,32,256]{2,1,0:T(8,128)(2,1)}), bf16[4,32,256]{2,1,0:T(8,128)(2,1)S(1)}, u32[]{:S(2)}, u32[]{:S(2)}) async-start(bf16[4,32,256]{2,1,0:T(8,128)(2,1)} %bitcast.9), calls=%async_computation.1 | async-start | bytes 131072 | tf_op jit(solution)/shard_map/all_to_all | solution.py:205
  88.5 9.8 %all-to-all-start = ((bf16[4,32,256]{2,1,0:T(8,128)(2,1)}), bf16[4,32,256]{2,1,0:T(8,128)(2,1)S(1)}, u32[]{:S(2)}, u32[]{:S(2)}) async-start(bf16[4,32,256]{2,1,0:T(8,128)(2,1)} %bitcast.7), calls=%async_computation | async-start | bytes 131072 | tf_op jit(solution)/shard_map/all_to_all | solution.py:204
  121.8 1.6 copy-start
  187.4 9.0 %all-to-all-start.3 = ((f32[128,2,4,16]{0,3,1,2:T(8,128)}), f32[128,2,4,16]{0,3,1,2:T(8,128)S(1)}, u32[]{:S(2)}, u32[]{:S(2)}) async-start(f32[128,2,4,16]{0,3,1,2:T(8,128)} %copy.50), calls=%async_computation.3 | async-start | bytes 131072 | tf_op jit(solution)/shard_map/all_to_all | solution.py:226
  196.4 56.1 %all-to-all-start.2 = ((bf16[128,4,2048]{2,0,1:T(8,128)(2,1)}), bf16[128,4,2048]{2,0,1:T(8,128)(2,1)S(1)}, u32[]{:S(2)}, u32[]{:S(2)}) async-start(bf16[128,4,2048]{2,0,1:T(8,128)(2,1)} %bitcast.118), calls=%async_computation.2 | async-start | bytes 4194304 | tf_op jit(solution)/shard_map/all_to_all | solution.py:223
  273.2 10.4 %all-to-all-start.5 = ((bf16[128,4,16]{0,2,1:T(8,128)(2,1)}), bf16[128,4,16]{0,2,1:T(8,128)(2,1)S(1)}, u32[]{:S(2)}, u32[]{:S(2)}) async-start(bf16[128,4,16]{0,2,1:T(8,128)(2,1)} %bitcast.18), calls=%async_computation.5 | async-start | bytes 32768 | tf_op jit(solution)/shard_map/all_to_all | solution.py:243
  283.6 49.8 %all-to-all-start.4 = ((bf16[128,64,128]{0,2,1:T(8,128)(2,1)}), bf16[128,64,128]{0,2,1:T(8,128)(2,1)S(1)}, u32[]{:S(2)}, u32[]{:S(2)}) async-start(bf16[128,64,128]{0,2,1:T(8,128)(2,1)} %divide_convert_fusion), calls=%async_computation.4 | async-start | bytes 4194304 | tf_op jit(solution)/shard_map/all_to_all | solution.py:242
Sparse Core Ops, SparseCore 0:
  11.0 47.1 all-gather.2
  74.3 47.4 all-gather.4
